TPU v7x, 32 devices: a whole 2x2x4 slice. The times are simulated.
32 devices in a mesh: grp: 4 (over y, core), dev: 8 (over z, x).
Axes of the slice: x: 2, y: 2, z: 4, core: 2. Of those that a mesh axis runs over, the one named last changes fastest.
Arguments:
- queries: bfloat16 [3072, 1024], P('dev'), may hold values from -16 to 16
- docs: bfloat16 [4096, 1024], P(('grp', 'dev')), may hold values from -16 to 16
- compat: int32 [24, 32], P('dev', 'grp'), may hold values from 0 to 1, as said below
- positives: int32 [3072], P('dev'), may hold values from 0 to 4095, as said below
Outputs:
- loss: float32 [3072], P('dev')
- query_grad: float32 [3072, 1024], P('dev')
- doc_grad: float32 [4096, 1024], P(('grp', 'dev'))
Inputs may be any that keep to these rules, and one draw needn't show every extreme that they name: compat[b, b % 32] is 1 for every query block b. positives[i] lies in a document block that is compatible with the block of query i.
All inputs are finite; a program needn't handle non-finite values.
Results may differ from a plain program's by a relative error of at most 0.0007.
Values may be sent and summed in bfloat16 or wider, within the bound.
A program may use at most 128 MiB of HBM per device.

v0:
```python
import jax
import jax.numpy as jnp
from jax import lax
from jax.sharding import PartitionSpec as P

BLOCK = 128
LOGIT_SCALE = 0.1
NEG_FLOOR = -1e30


def joined(value, axis, combine):
    everything = jax.tree.map(lambda part: lax.all_gather(part, axis), value)
    first = jax.tree.map(lambda part: part[0], everything)

    def hop(k, so_far):
        return combine(so_far, jax.tree.map(lambda part: part[k], everything))

    return lax.fori_loop(1, lax.axis_size(axis), hop, first)


def from_behind(value, axis, by):
    devices = lax.axis_size(axis)
    return lax.ppermute(value, axis, [(i, (i + by) % devices) for i in range(devices)])


def panel_scores(queries, panel):
    return LOGIT_SCALE * lax.dot_general(
        queries, panel, (((1,), (1,)), ((), ())), preferred_element_type=jnp.float32
    )


def panel_masks(compat, positives, column_start, doc_offset, block, panel_rows):
    blocks = lax.dynamic_slice_in_dim(compat, column_start, panel_rows // block, 1)
    live = jnp.repeat(jnp.repeat(blocks, block, axis=0), block, axis=1) > 0
    doc_ids = doc_offset + jnp.arange(panel_rows, dtype=jnp.int32)
    target = doc_ids[None, :] == positives[:, None]
    return (live, target)


def add_stats(stats, scores, live, target):
    row_max, total, chosen = stats
    local_max = jnp.max(jnp.where(live, scores, NEG_FLOOR), axis=1)
    new_max = jnp.maximum(row_max, local_max)
    terms = jnp.where(live, jnp.exp(scores - new_max[:, None]), 0.0)
    total = total * jnp.exp(row_max - new_max) + jnp.sum(terms, axis=1)
    chosen = chosen + jnp.sum(jnp.where(target, scores, 0.0), axis=1)
    return (new_max, total, chosen)


def merge_stats(first, second):
    top = jnp.maximum(first[0], second[0])
    total = first[1] * jnp.exp(first[0] - top) + second[1] * jnp.exp(second[0] - top)
    return (top, total, first[2] + second[2])


def finish_stats(stats):
    row_max, total, chosen = joined(stats, "grp", merge_stats)
    lse = row_max + jnp.log(total)
    return (lse, lse - chosen)


def coefficients(scores, live, target, lse):
    prob = jnp.where(live, jnp.exp(scores - lse[:, None]), 0.0)
    return (prob - target.astype(jnp.float32)).astype(jnp.bfloat16)


def local(queries, docs, compat, positives):
    width = lax.axis_size("dev")
    position = lax.axis_index("dev")
    group_index = lax.axis_index("grp")
    block = BLOCK
    panel_rows = docs.shape[0]
    query_rows = queries.shape[0]
    panel_blocks = panel_rows // block
    group_start = group_index * (width * panel_rows)
    empty_stats = (
        jnp.full((query_rows,), NEG_FLOOR, jnp.float32),
        jnp.zeros((query_rows,), jnp.float32),
        jnp.zeros((query_rows,), jnp.float32),
    )

    def masks_for(owner):
        return panel_masks(
            compat,
            positives,
            owner * panel_blocks,
            group_start + owner * panel_rows,
            block,
            panel_rows,
        )

    def visit(stats, panel, owner):
        live, target = masks_for(owner)
        scores = panel_scores(queries, panel)
        return (add_stats(stats, scores, live, target), scores)

    def gradient_step(carry, panel, scores, owner, lse):
        live, target = masks_for(owner)
        query_sum, doc_sum = carry
        coef = coefficients(scores, live, target, lse)
        query_sum = query_sum + LOGIT_SCALE * jnp.dot(
            coef, panel, preferred_element_type=jnp.float32
        )
        doc_sum = doc_sum + LOGIT_SCALE * lax.dot_general(
            coef, queries, (((0,), (0,)), ((), ())), preferred_element_type=jnp.float32
        )
        return (query_sum, doc_sum)

    stats, first_scores = visit(empty_stats, docs, position)
    store = jnp.zeros((width,) + docs.shape, docs.dtype).at[0].set(docs)
    score_store = jnp.zeros((width, query_rows, panel_rows), jnp.float32).at[0].set(first_scores)

    def first_turn(turn_index, carry):
        current, kept, kept_scores, partial_value = carry
        current = from_behind(current, "dev", 1)
        owner = (position - turn_index) % width
        kept = lax.dynamic_update_index_in_dim(kept, current, turn_index, 0)
        partial_value, scores = visit(partial_value, current, owner)
        kept_scores = lax.dynamic_update_index_in_dim(kept_scores, scores, turn_index, 0)
        return (current, kept, kept_scores, partial_value)

    current, store, score_store, stats = lax.fori_loop(
        1, width, first_turn, (docs, store, score_store, stats)
    )
    lse, loss = finish_stats(stats)
    start_carry = (
        jnp.zeros((query_rows, docs.shape[1]), jnp.float32),
        jnp.zeros((panel_rows, docs.shape[1]), jnp.float32),
    )
    start_carry = gradient_step(start_carry, docs, score_store[0], position, lse)

    def second_turn(turn_index, carry):
        query_sum, doc_sum = carry
        doc_sum = from_behind(doc_sum, "dev", 1)
        owner = (position - turn_index) % width
        panel = lax.dynamic_index_in_dim(store, turn_index, 0, keepdims=False)
        scores = lax.dynamic_index_in_dim(score_store, turn_index, 0, keepdims=False)
        return gradient_step((query_sum, doc_sum), panel, scores, owner, lse)

    query_part, doc_part = lax.fori_loop(1, width, second_turn, start_carry)
    doc_grad = from_behind(doc_part, "dev", 1)
    query_grad = lax.psum(query_part, "grp")
    return (loss, query_grad, doc_grad)


def solution(mesh):
    return jax.shard_map(
        local,
        mesh=mesh,
        in_specs=(P("dev", None), P(("grp", "dev"), None), P("dev", "grp"), P("dev")),
        out_specs=(P("dev"), P("dev", None), P(("grp", "dev"), None)),
        check_vma=False,
    )
```

profile of v0, /device:TPU:0, one launch (start us, length us, event | category | flops | bytes accessed | tf_op | source)
XLA Modules:
  0.0 280.5 jit_solution(13684167352823001613)
XLA Ops:
  14.8 83.8 %while.67 = (s32[]{:T(128)}, bf16[128,1024]{1,0:T(8,128)(2,1)}, bf16[8,128,1024]{2,1,0:T(8,128)(2,1)S(1)}, f32[8,384,128]{1,2,0:T(8,128)}, f32[384]{0:T(512)S(1)...) while((s32[]{:T(128)}, bf16[128,1024]{1,0:T(8,128)(2,1)}, ...), condition=%wide.region_7.8_spmd, body=%wide.region_3.7_spmd.sunk | while | flops 101106560 | bytes 3962444 | solution.py:122
  14.8 2.9 %collective-permute-start = (bf16[128,1024]{1,0:T(8,128)(2,1)}, bf16[128,1024]{1,0:T(8,128)(2,1)S(1)}, u32[]{:S(2)}, u32[]{:S(2)}) collective-permute-start(bf16[128,1024]{1,0:T(8,128)(2,1)} %get-tuple-element.1277), channel_id=1, source_target_pairs={{0,1},{1,2},{2,3},{3,4},{4,5},{5,6},{6,7},{7,0},{8,9},{9,10},{10,1... | collective-permute-start | bytes 786440 | tf_op jit(solution)/shard_map/while/body/eval_jaxpr/ppermute | solution.py:23
  17.8 9.5 %collective-permute-done = bf16[128,1024]{1,0:T(8,128)(2,1)S(1)} collective-permute-done((bf16[128,1024]{1,0:T(8,128)(2,1)}, bf16[128,1024]{1,0:T(8,128)(2,1)S(1)}, u32[]{:S(2)}, u32[]{:S(2)}) %collective-permute-start) | collective-permute-done | bytes 262176 | tf_op jit(solution)/shard_map/while/body/eval_jaxpr/ppermute | solution.py:23
  29.5 10.2 %collective-permute-done = bf16[128,1024]{1,0:T(8,128)(2,1)S(1)} collective-permute-done((bf16[128,1024]{1,0:T(8,128)(2,1)}, bf16[128,1024]{1,0:T(8,128)(2,1)S(1)}, u32[]{:S(2)}, u32[]{:S(2)}) %collective-permute-start) | collective-permute-done | bytes 262176 | tf_op jit(solution)/shard_map/while/body/eval_jaxpr/ppermute | solution.py:23
  41.9 9.3 %collective-permute-done = bf16[128,1024]{1,0:T(8,128)(2,1)S(1)} collective-permute-done((bf16[128,1024]{1,0:T(8,128)(2,1)}, bf16[128,1024]{1,0:T(8,128)(2,1)S(1)}, u32[]{:S(2)}, u32[]{:S(2)}) %collective-permute-start) | collective-permute-done | bytes 262176 | tf_op jit(solution)/shard_map/while/body/eval_jaxpr/ppermute | solution.py:23
  53.4 9.1 %collective-permute-done = bf16[128,1024]{1,0:T(8,128)(2,1)S(1)} collective-permute-done((bf16[128,1024]{1,0:T(8,128)(2,1)}, bf16[128,1024]{1,0:T(8,128)(2,1)S(1)}, u32[]{:S(2)}, u32[]{:S(2)}) %collective-permute-start) | collective-permute-done | bytes 262176 | tf_op jit(solution)/shard_map/while/body/eval_jaxpr/ppermute | solution.py:23
  64.8 9.1 %collective-permute-done = bf16[128,1024]{1,0:T(8,128)(2,1)S(1)} collective-permute-done((bf16[128,1024]{1,0:T(8,128)(2,1)}, bf16[128,1024]{1,0:T(8,128)(2,1)S(1)}, u32[]{:S(2)}, u32[]{:S(2)}) %collective-permute-start) | collective-permute-done | bytes 262176 | tf_op jit(solution)/shard_map/while/body/eval_jaxpr/ppermute | solution.py:23
  76.1 9.1 %collective-permute-done = bf16[128,1024]{1,0:T(8,128)(2,1)S(1)} collective-permute-done((bf16[128,1024]{1,0:T(8,128)(2,1)}, bf16[128,1024]{1,0:T(8,128)(2,1)S(1)}, u32[]{:S(2)}, u32[]{:S(2)}) %collective-permute-start) | collective-permute-done | bytes 262176 | tf_op jit(solution)/shard_map/while/body/eval_jaxpr/ppermute | solution.py:23
  87.4 9.1 %collective-permute-done = bf16[128,1024]{1,0:T(8,128)(2,1)S(1)} collective-permute-done((bf16[128,1024]{1,0:T(8,128)(2,1)}, bf16[128,1024]{1,0:T(8,128)(2,1)S(1)}, u32[]{:S(2)}, u32[]{:S(2)}) %collective-permute-start) | collective-permute-done | bytes 262176 | tf_op jit(solution)/shard_map/while/body/eval_jaxpr/ppermute | solution.py:23
  98.5 5.2 %all-gather.5 = f32[4,1,384]{2,1,0:T(1,128)S(1)} all-gather(f32[1,1,384]{2,1,0:T(1,128)S(1)} %reshape.269), channel_id=4, replica_groups=mesh['grp'=4,'dev'=8] {'grp'}, dimensions={0}, use_global_device_ids=true | all-gather | bytes 7680 | tf_op jit(solution)/shard_map/all_gather | solution.py:12
  103.7 5.2 %all-gather.4 = f32[4,1,384]{2,1,0:T(1,128)S(1)} all-gather(f32[1,1,384]{2,1,0:T(1,128)S(1)} %reshape.267), channel_id=3, replica_groups=mesh['grp'=4,'dev'=8] {'grp'}, dimensions={0}, use_global_device_ids=true | all-gather | bytes 7680 | tf_op jit(solution)/shard_map/all_gather | solution.py:12
  108.9 5.2 %all-gather.3 = f32[4,1,384]{2,1,0:T(1,128)S(1)} all-gather(f32[1,1,384]{2,1,0:T(1,128)S(1)} %reshape.265), channel_id=2, replica_groups=mesh['grp'=4,'dev'=8] {'grp'}, dimensions={0}, use_global_device_ids=true | all-gather | bytes 7680 | tf_op jit(solution)/shard_map/all_gather | solution.py:12
  115.0 2.1 convolution_multiply_fusion.3
  118.5 110.6 %while.69 = (s32[]{:T(128)}, f32[384,1024]{1,0:T(8,128)S(1)}, f32[128,1024]{1,0:T(8,128)}, s32[]{:T(128)}, s32[3,8]{0,1:T(8,128)S(1)}, /*index=5*/f32[8,384,128]...) while((s32[]{:T(128)}, f32[384,1024]{1,0:T(8,128)S(1)}, ...), condition=%wide.region_11.12_spmd, body=%wide.region_10.11_spmd.sunk | while | flops 202965152 | bytes 8528964 | solution.py:140
  121.2 14.3 %collective-permute-done.1 = f32[128,1024]{1,0:T(8,128)S(1)} collective-permute-done((f32[128,1024]{1,0:T(8,128)}, f32[128,1024]{1,0:T(8,128)S(1)}, u32[]{:S(2)}, u32[]{:S(2)}) %collective-permute-start.1) | collective-permute-done | bytes 524320 | tf_op jit(solution)/shard_map/while/body/eval_jaxpr/ppermute | solution.py:23
  139.6 13.6 %collective-permute-done.1 = f32[128,1024]{1,0:T(8,128)S(1)} collective-permute-done((f32[128,1024]{1,0:T(8,128)}, f32[128,1024]{1,0:T(8,128)S(1)}, u32[]{:S(2)}, u32[]{:S(2)}) %collective-permute-start.1) | collective-permute-done | bytes 524320 | tf_op jit(solution)/shard_map/while/body/eval_jaxpr/ppermute | solution.py:23
  157.2 12.7 %collective-permute-done.1 = f32[128,1024]{1,0:T(8,128)S(1)} collective-permute-done((f32[128,1024]{1,0:T(8,128)}, f32[128,1024]{1,0:T(8,128)S(1)}, u32[]{:S(2)}, u32[]{:S(2)}) %collective-permute-start.1) | collective-permute-done | bytes 524320 | tf_op jit(solution)/shard_map/while/body/eval_jaxpr/ppermute | solution.py:23
  173.8 11.7 %collective-permute-done.1 = f32[128,1024]{1,0:T(8,128)S(1)} collective-permute-done((f32[128,1024]{1,0:T(8,128)}, f32[128,1024]{1,0:T(8,128)S(1)}, u32[]{:S(2)}, u32[]{:S(2)}) %collective-permute-start.1) | collective-permute-done | bytes 524320 | tf_op jit(solution)/shard_map/while/body/eval_jaxpr/ppermute | solution.py:23
  189.5 10.8 %collective-permute-done.1 = f32[128,1024]{1,0:T(8,128)S(1)} collective-permute-done((f32[128,1024]{1,0:T(8,128)}, f32[128,1024]{1,0:T(8,128)S(1)}, u32[]{:S(2)}, u32[]{:S(2)}) %collective-permute-start.1) | collective-permute-done | bytes 524320 | tf_op jit(solution)/shard_map/while/body/eval_jaxpr/ppermute | solution.py:23
  204.4 9.9 %collective-permute-done.1 = f32[128,1024]{1,0:T(8,128)S(1)} collective-permute-done((f32[128,1024]{1,0:T(8,128)}, f32[128,1024]{1,0:T(8,128)S(1)}, u32[]{:S(2)}, u32[]{:S(2)}) %collective-permute-start.1) | collective-permute-done | bytes 524320 | tf_op jit(solution)/shard_map/while/body/eval_jaxpr/ppermute | solution.py:23
  218.3 9.4 %collective-permute-done.1 = f32[128,1024]{1,0:T(8,128)S(1)} collective-permute-done((f32[128,1024]{1,0:T(8,128)}, f32[128,1024]{1,0:T(8,128)S(1)}, u32[]{:S(2)}, u32[]{:S(2)}) %collective-permute-start.1) | collective-permute-done | bytes 524320 | tf_op jit(solution)/shard_map/while/body/eval_jaxpr/ppermute | solution.py:23
  230.4 11.9 %collective-permute-done.2 = f32[128,1024]{1,0:T(8,128)S(1)} collective-permute-done((f32[128,1024]{1,0:T(8,128)S(1)}, f32[128,1024]{1,0:T(8,128)S(1)}, u32[]{:S(2)}, u32[]{:S(2)}) %collective-permute-start.2) | collective-permute-done | bytes 524320 | tf_op jit(solution)/shard_map/ppermute | solution.py:23
  242.3 27.8 %all-reduce.4.cloned.1.call-done = f32[384,1024]{1,0:T(8,128)} async-done(((f32[384,1024]{1,0:T(8,128)}), f32[384,1024]{1,0:T(8,128)}) %all-reduce.4.cloned.1.call-update) | async-done | bytes 1572880 | tf_op jit(solution)/shard_map/psum | solution.py:142
  270.1 2.7 copy.71
  (197 shorter events, 54.8 us)
Async XLA Ops:
  7.2 5.1 %copy-start.4 = (s32[384]{0:T(512)S(1)}, s32[384]{0:T(512)}, u32[]{:S(2)}) copy-start(s32[384]{0:T(512)} %param.17) | copy-start | bytes 4612
  7.2 262.9 %all-reduce.4.cloned.1.call-start = ((), (), s32[]{:S(2)}) async-start(), calls=%async_computation | async-start | bytes 3145728 | tf_op jit(solution)/shard_map/psum | solution.py:142
  10.6 3.0 %copy-start.3 = (bf16[128,1024]{1,0:T(8,128)(2,1)S(1)}, bf16[128,1024]{1,0:T(8,128)(2,1)}, u32[]{:S(2)}) copy-start(bf16[128,1024]{1,0:T(8,128)(2,1)} %param.15) | copy-start | bytes 786436
  13.6 1.1 copy-start
  14.8 12.5 %collective-permute-start = (bf16[128,1024]{1,0:T(8,128)(2,1)}, bf16[128,1024]{1,0:T(8,128)(2,1)S(1)}, u32[]{:S(2)}, u32[]{:S(2)}) collective-permute-start(bf16[128,1024]{1,0:T(8,128)(2,1)} %get-tuple-element.1277), channel_id=1, source_target_pairs={{0,1},{1,2},{2,3},{3,4},{4,5},{5,6},{6,7},{7,0},{8,9},{9,10},{10,1... | collective-permute-start | bytes 786440 | tf_op jit(solution)/shard_map/while/body/eval_jaxpr/ppermute | solution.py:23
  29.2 10.4 %collective-permute-start = (bf16[128,1024]{1,0:T(8,128)(2,1)}, bf16[128,1024]{1,0:T(8,128)(2,1)S(1)}, u32[]{:S(2)}, u32[]{:S(2)}) collective-permute-start(bf16[128,1024]{1,0:T(8,128)(2,1)} %get-tuple-element.1277), channel_id=1, source_target_pairs={{0,1},{1,2},{2,3},{3,4},{4,5},{5,6},{6,7},{7,0},{8,9},{9,10},{10,1... | collective-permute-start | bytes 786440 | tf_op jit(solution)/shard_map/while/body/eval_jaxpr/ppermute | solution.py:23
  41.7 9.5 %collective-permute-start = (bf16[128,1024]{1,0:T(8,128)(2,1)}, bf16[128,1024]{1,0:T(8,128)(2,1)S(1)}, u32[]{:S(2)}, u32[]{:S(2)}) collective-permute-start(bf16[128,1024]{1,0:T(8,128)(2,1)} %get-tuple-element.1277), channel_id=1, source_target_pairs={{0,1},{1,2},{2,3},{3,4},{4,5},{5,6},{6,7},{7,0},{8,9},{9,10},{10,1... | collective-permute-start | bytes 786440 | tf_op jit(solution)/shard_map/while/body/eval_jaxpr/ppermute | solution.py:23
  53.2 9.3 %collective-permute-start = (bf16[128,1024]{1,0:T(8,128)(2,1)}, bf16[128,1024]{1,0:T(8,128)(2,1)S(1)}, u32[]{:S(2)}, u32[]{:S(2)}) collective-permute-start(bf16[128,1024]{1,0:T(8,128)(2,1)} %get-tuple-element.1277), channel_id=1, source_target_pairs={{0,1},{1,2},{2,3},{3,4},{4,5},{5,6},{6,7},{7,0},{8,9},{9,10},{10,1... | collective-permute-start | bytes 786440 | tf_op jit(solution)/shard_map/while/body/eval_jaxpr/ppermute | solution.py:23
  64.5 9.3 %collective-permute-start = (bf16[128,1024]{1,0:T(8,128)(2,1)}, bf16[128,1024]{1,0:T(8,128)(2,1)S(1)}, u32[]{:S(2)}, u32[]{:S(2)}) collective-permute-start(bf16[128,1024]{1,0:T(8,128)(2,1)} %get-tuple-element.1277), channel_id=1, source_target_pairs={{0,1},{1,2},{2,3},{3,4},{4,5},{5,6},{6,7},{7,0},{8,9},{9,10},{10,1... | collective-permute-start | bytes 786440 | tf_op jit(solution)/shard_map/while/body/eval_jaxpr/ppermute | solution.py:23
  75.9 9.3 %collective-permute-start = (bf16[128,1024]{1,0:T(8,128)(2,1)}, bf16[128,1024]{1,0:T(8,128)(2,1)S(1)}, u32[]{:S(2)}, u32[]{:S(2)}) collective-permute-start(bf16[128,1024]{1,0:T(8,128)(2,1)} %get-tuple-element.1277), channel_id=1, source_target_pairs={{0,1},{1,2},{2,3},{3,4},{4,5},{5,6},{6,7},{7,0},{8,9},{9,10},{10,1... | collective-permute-start | bytes 786440 | tf_op jit(solution)/shard_map/while/body/eval_jaxpr/ppermute | solution.py:23
  87.2 9.3 %collective-permute-start = (bf16[128,1024]{1,0:T(8,128)(2,1)}, bf16[128,1024]{1,0:T(8,128)(2,1)S(1)}, u32[]{:S(2)}, u32[]{:S(2)}) collective-permute-start(bf16[128,1024]{1,0:T(8,128)(2,1)} %get-tuple-element.1277), channel_id=1, source_target_pairs={{0,1},{1,2},{2,3},{3,4},{4,5},{5,6},{6,7},{7,0},{8,9},{9,10},{10,1... | collective-permute-start | bytes 786440 | tf_op jit(solution)/shard_map/while/body/eval_jaxpr/ppermute | solution.py:23
  98.5 16.5 %copy-start.2 = (bf16[8,128,1024]{2,1,0:T(8,128)(2,1)}, bf16[8,128,1024]{2,1,0:T(8,128)(2,1)S(1)}, u32[]{:S(2)}) copy-start(bf16[8,128,1024]{2,1,0:T(8,128)(2,1)S(1)} %get-tuple-element.1351) | copy-start | bytes 6291460
  118.5 17.1 %collective-permute-start.1 = (f32[128,1024]{1,0:T(8,128)}, f32[128,1024]{1,0:T(8,128)S(1)}, u32[]{:S(2)}, u32[]{:S(2)}) collective-permute-start(f32[128,1024]{1,0:T(8,128)} %get-tuple-element.1361), channel_id=1, source_target_pairs={{0,1},{1,2},{2,3},{3,4},{4,5},{5,6},{6,7},{7,0},{8,9},{9,10},{10,1... | collective-permute-start | bytes 1572872 | tf_op jit(solution)/shard_map/while/body/eval_jaxpr/ppermute | solution.py:23
  136.9 16.2 %collective-permute-start.1 = (f32[128,1024]{1,0:T(8,128)}, f32[128,1024]{1,0:T(8,128)S(1)}, u32[]{:S(2)}, u32[]{:S(2)}) collective-permute-start(f32[128,1024]{1,0:T(8,128)} %get-tuple-element.1361), channel_id=1, source_target_pairs={{0,1},{1,2},{2,3},{3,4},{4,5},{5,6},{6,7},{7,0},{8,9},{9,10},{10,1... | collective-permute-start | bytes 1572872 | tf_op jit(solution)/shard_map/while/body/eval_jaxpr/ppermute | solution.py:23
  154.5 15.3 %collective-permute-start.1 = (f32[128,1024]{1,0:T(8,128)}, f32[128,1024]{1,0:T(8,128)S(1)}, u32[]{:S(2)}, u32[]{:S(2)}) collective-permute-start(f32[128,1024]{1,0:T(8,128)} %get-tuple-element.1361), channel_id=1, source_target_pairs={{0,1},{1,2},{2,3},{3,4},{4,5},{5,6},{6,7},{7,0},{8,9},{9,10},{10,1... | collective-permute-start | bytes 1572872 | tf_op jit(solution)/shard_map/while/body/eval_jaxpr/ppermute | solution.py:23
  171.2 14.4 %collective-permute-start.1 = (f32[128,1024]{1,0:T(8,128)}, f32[128,1024]{1,0:T(8,128)S(1)}, u32[]{:S(2)}, u32[]{:S(2)}) collective-permute-start(f32[128,1024]{1,0:T(8,128)} %get-tuple-element.1361), channel_id=1, source_target_pairs={{0,1},{1,2},{2,3},{3,4},{4,5},{5,6},{6,7},{7,0},{8,9},{9,10},{10,1... | collective-permute-start | bytes 1572872 | tf_op jit(solution)/shard_map/while/body/eval_jaxpr/ppermute | solution.py:23
  186.9 13.5 %collective-permute-start.1 = (f32[128,1024]{1,0:T(8,128)}, f32[128,1024]{1,0:T(8,128)S(1)}, u32[]{:S(2)}, u32[]{:S(2)}) collective-permute-start(f32[128,1024]{1,0:T(8,128)} %get-tuple-element.1361), channel_id=1, source_target_pairs={{0,1},{1,2},{2,3},{3,4},{4,5},{5,6},{6,7},{7,0},{8,9},{9,10},{10,1... | collective-permute-start | bytes 1572872 | tf_op jit(solution)/shard_map/while/body/eval_jaxpr/ppermute | solution.py:23
  201.7 12.5 %collective-permute-start.1 = (f32[128,1024]{1,0:T(8,128)}, f32[128,1024]{1,0:T(8,128)S(1)}, u32[]{:S(2)}, u32[]{:S(2)}) collective-permute-start(f32[128,1024]{1,0:T(8,128)} %get-tuple-element.1361), channel_id=1, source_target_pairs={{0,1},{1,2},{2,3},{3,4},{4,5},{5,6},{6,7},{7,0},{8,9},{9,10},{10,1... | collective-permute-start | bytes 1572872 | tf_op jit(solution)/shard_map/while/body/eval_jaxpr/ppermute | solution.py:23
  215.6 12.1 %collective-permute-start.1 = (f32[128,1024]{1,0:T(8,128)}, f32[128,1024]{1,0:T(8,128)S(1)}, u32[]{:S(2)}, u32[]{:S(2)}) collective-permute-start(f32[128,1024]{1,0:T(8,128)} %get-tuple-element.1361), channel_id=1, source_target_pairs={{0,1},{1,2},{2,3},{3,4},{4,5},{5,6},{6,7},{7,0},{8,9},{9,10},{10,1... | collective-permute-start | bytes 1572872 | tf_op jit(solution)/shard_map/while/body/eval_jaxpr/ppermute | solution.py:23
  229.0 1.1 copy-start.1
  229.0 1.4 copy-start.5
  230.4 11.9 %collective-permute-start.2 = (f32[128,1024]{1,0:T(8,128)S(1)}, f32[128,1024]{1,0:T(8,128)S(1)}, u32[]{:S(2)}, u32[]{:S(2)}) collective-permute-start(f32[128,1024]{1,0:T(8,128)S(1)} %copy-done.5), channel_id=1, source_target_pairs={{0,1},{1,2},{2,3},{3,4},{4,5},{5,6},{6,7},{7,0},{8,9},{9,10},{10,1... | collective-permute-start | bytes 1572872 | tf_op jit(solution)/shard_map/ppermute | solution.py:23
Sparse Core Ops, SparseCore 0:
  230.3 39.7 all-reduce.3
where the time goes:
time: 281 us; the launch traced here: 280 us
  waiting for transfers between devices  188 us (67%)
  matrix products  32.2 us (11%)
  local copies, waits for them, and re-layouts  23.6 us (8%)
  blocking collectives  15.5 us (6%)
  between operations  14.1 us (5%)
  starting transfers between devices  3.4 us (1%)
  other arithmetic  3.12 us (1%)
    ppermute x15, waiting for transfers between devices, from_behind(): lax.ppermute(value, axis, [(i, (i + by) % devices) for i in range(devices)])  160 us
    psum x1, waiting for transfers between devices, local(): query_grad = lax.psum(query_part, 'grp')  27.8 us
    all_gather x3, blocking collectives, joined(): everything = jax.tree.map(lambda part: lax.all_gather(part, axis), value)  15.5 us
    dot_general x8, matrix products, gradient_step(): jnp.dot(coef, panel, preferred_element_type=jnp.float32)  11.7 us
    dot_general x8, matrix products, gradient_step(): lax.dot_general(coef, queries, (((0,), (0,)), ((), ())), preferred_elemen...  11.5 us
    dot_general x8, matrix products, panel_scores(): lax.dot_general(queries, panel, (((1,), (1,)), ((), ())), preferred_eleme...  9 us
    unnamed x21, local copies, waits for them, and re-layouts  7.47 us
    dynamic_slice x14, local copies, waits for them, and re-layouts, second_turn(): lax.dynamic_index_in_dim(score_store, turn_index, 0, keepdims=False)  7.44 us
  transfers between devices with their start and end apart: 16, of which 16 were waited for; matrix products, arithmetic and copies ran while one was open for 7% of the time, Pallas kernels for 0%

commit v1 on v0

--- a/solution.py
+++ b/solution.py
@@ -139,7 +139,11 @@
 
     query_part, doc_part = lax.fori_loop(1, width, second_turn, start_carry)
     doc_grad = from_behind(doc_part, "dev", 1)
-    query_grad = lax.psum(query_part, "grp")
+    query_grad = query_part
+    for hop_ in (1, 2):
+        query_grad = query_grad + lax.ppermute(
+            query_grad, "grp", [(dev, dev ^ hop_) for dev in range(4)]
+        )
     return (loss, query_grad, doc_grad)
 
 

time: 281 us -> 266 us (0.947)
  between operations: 14.1 us -> 0.76 us
  local copies, waits for them, and re-layouts: 23.6 us -> 19.5 us
    psum x1 -> x0, waiting for transfers between devices: 27.8 us -> none  [local(): query_grad = lax.psum(query_part, 'grp')]
    ppermute x0 -> x2, waiting for transfers between devices: none -> 22.4 us  [local(): lax.ppermute(query_grad, 'grp', [(dev, dev ^ hop_) for dev in range(4)])]
    ppermute x15, waiting for transfers between devices: 160 us -> 164 us  [from_behind(): lax.ppermute(value, axis, [(i, (i + by) % devices) for i in range(devices)])]
    unnamed x21 -> x18, local copies, waits for them, and re-layouts: 7.47 us -> 3.37 us
  transfers between devices with their start and end apart: 16 -> 17, of which waited for: 16 -> 17; matrix products, arithmetic and copies ran while one was open for 7% -> 7% of each run, Pallas kernels for 0% -> 0%
where the time goes in v1:
time: 266 us; the launch traced here: 265 us
  waiting for transfers between devices  187 us (70%)
  matrix products  32.2 us (12%)
  local copies, waits for them, and re-layouts  19.5 us (7%)
  blocking collectives  15.5 us (6%)
  other arithmetic  4.81 us (2%)
  starting transfers between devices  4.5 us (2%)
    ppermute x15, waiting for transfers between devices, from_behind(): lax.ppermute(value, axis, [(i, (i + by) % devices) for i in range(devices)])  164 us
    ppermute x2, waiting for transfers between devices, local(): lax.ppermute(query_grad, 'grp', [(dev, dev ^ hop_) for dev in range(4)])  22.4 us
    all_gather x3, blocking collectives, joined(): everything = jax.tree.map(lambda part: lax.all_gather(part, axis), value)  15.5 us
    dot_general x8, matrix products, gradient_step(): jnp.dot(coef, panel, preferred_element_type=jnp.float32)  11.7 us
    dot_general x8, matrix products, gradient_step(): lax.dot_general(coef, queries, (((0,), (0,)), ((), ())), preferred_elemen...  11.5 us
    dot_general x8, matrix products, panel_scores(): lax.dot_general(queries, panel, (((1,), (1,)), ((), ())), preferred_eleme...  9 us
    dynamic_slice x14, local copies, waits for them, and re-layouts, second_turn(): lax.dynamic_index_in_dim(score_store, turn_index, 0, keepdims=False)  7.44 us
  transfers between devices with their start and end apart: 17, of which 17 were waited for; matrix products, arithmetic and copies ran while one was open for 7% of the time, Pallas kernels for 0%

profile of v1, /device:TPU:0, one launch (start us, length us, event | category | flops | bytes accessed | tf_op | source)
XLA Modules:
  0.0 264.9 jit_solution(1222197388995258729)
XLA Ops:
  8.2 83.8 %while.67 = (s32[]{:T(128)}, bf16[128,1024]{1,0:T(8,128)(2,1)}, bf16[8,128,1024]{2,1,0:T(8,128)(2,1)S(1)}, f32[8,384,128]{1,2,0:T(8,128)}, f32[384]{0:T(512)S(1)...) while((s32[]{:T(128)}, bf16[128,1024]{1,0:T(8,128)(2,1)}, ...), condition=%wide.region_7.8_spmd, body=%wide.region_3.7_spmd.sunk | while | flops 101106560 | bytes 3962444 | solution.py:122
  8.2 2.9 %collective-permute-start = (bf16[128,1024]{1,0:T(8,128)(2,1)}, bf16[128,1024]{1,0:T(8,128)(2,1)S(1)}, u32[]{:S(2)}, u32[]{:S(2)}) collective-permute-start(bf16[128,1024]{1,0:T(8,128)(2,1)} %get-tuple-element.1277), channel_id=1, source_target_pairs={{0,1},{1,2},{2,3},{3,4},{4,5},{5,6},{6,7},{7,0},{8,9},{9,10},{10,1... | collective-permute-start | bytes 786440 | tf_op jit(solution)/shard_map/while/body/eval_jaxpr/ppermute | solution.py:23
  11.2 9.5 %collective-permute-done = bf16[128,1024]{1,0:T(8,128)(2,1)S(1)} collective-permute-done((bf16[128,1024]{1,0:T(8,128)(2,1)}, bf16[128,1024]{1,0:T(8,128)(2,1)S(1)}, u32[]{:S(2)}, u32[]{:S(2)}) %collective-permute-start) | collective-permute-done | bytes 262176 | tf_op jit(solution)/shard_map/while/body/eval_jaxpr/ppermute | solution.py:23
  22.9 10.2 %collective-permute-done = bf16[128,1024]{1,0:T(8,128)(2,1)S(1)} collective-permute-done((bf16[128,1024]{1,0:T(8,128)(2,1)}, bf16[128,1024]{1,0:T(8,128)(2,1)S(1)}, u32[]{:S(2)}, u32[]{:S(2)}) %collective-permute-start) | collective-permute-done | bytes 262176 | tf_op jit(solution)/shard_map/while/body/eval_jaxpr/ppermute | solution.py:23
  35.3 9.3 %collective-permute-done = bf16[128,1024]{1,0:T(8,128)(2,1)S(1)} collective-permute-done((bf16[128,1024]{1,0:T(8,128)(2,1)}, bf16[128,1024]{1,0:T(8,128)(2,1)S(1)}, u32[]{:S(2)}, u32[]{:S(2)}) %collective-permute-start) | collective-permute-done | bytes 262176 | tf_op jit(solution)/shard_map/while/body/eval_jaxpr/ppermute | solution.py:23
  46.9 9.1 %collective-permute-done = bf16[128,1024]{1,0:T(8,128)(2,1)S(1)} collective-permute-done((bf16[128,1024]{1,0:T(8,128)(2,1)}, bf16[128,1024]{1,0:T(8,128)(2,1)S(1)}, u32[]{:S(2)}, u32[]{:S(2)}) %collective-permute-start) | collective-permute-done | bytes 262176 | tf_op jit(solution)/shard_map/while/body/eval_jaxpr/ppermute | solution.py:23
  58.2 9.1 %collective-permute-done = bf16[128,1024]{1,0:T(8,128)(2,1)S(1)} collective-permute-done((bf16[128,1024]{1,0:T(8,128)(2,1)}, bf16[128,1024]{1,0:T(8,128)(2,1)S(1)}, u32[]{:S(2)}, u32[]{:S(2)}) %collective-permute-start) | collective-permute-done | bytes 262176 | tf_op jit(solution)/shard_map/while/body/eval_jaxpr/ppermute | solution.py:23
  69.5 9.1 %collective-permute-done = bf16[128,1024]{1,0:T(8,128)(2,1)S(1)} collective-permute-done((bf16[128,1024]{1,0:T(8,128)(2,1)}, bf16[128,1024]{1,0:T(8,128)(2,1)S(1)}, u32[]{:S(2)}, u32[]{:S(2)}) %collective-permute-start) | collective-permute-done | bytes 262176 | tf_op jit(solution)/shard_map/while/body/eval_jaxpr/ppermute | solution.py:23
  80.9 9.1 %collective-permute-done = bf16[128,1024]{1,0:T(8,128)(2,1)S(1)} collective-permute-done((bf16[128,1024]{1,0:T(8,128)(2,1)}, bf16[128,1024]{1,0:T(8,128)(2,1)S(1)}, u32[]{:S(2)}, u32[]{:S(2)}) %collective-permute-start) | collective-permute-done | bytes 262176 | tf_op jit(solution)/shard_map/while/body/eval_jaxpr/ppermute | solution.py:23
  92.0 5.2 %all-gather.5 = f32[4,1,384]{2,1,0:T(1,128)S(1)} all-gather(f32[1,1,384]{2,1,0:T(1,128)S(1)} %reshape.269), channel_id=4, replica_groups=mesh['grp'=4,'dev'=8] {'grp'}, dimensions={0}, use_global_device_ids=true | all-gather | bytes 7680 | tf_op jit(solution)/shard_map/all_gather | solution.py:12
  97.2 5.2 %all-gather.4 = f32[4,1,384]{2,1,0:T(1,128)S(1)} all-gather(f32[1,1,384]{2,1,0:T(1,128)S(1)} %reshape.267), channel_id=3, replica_groups=mesh['grp'=4,'dev'=8] {'grp'}, dimensions={0}, use_global_device_ids=true | all-gather | bytes 7680 | tf_op jit(solution)/shard_map/all_gather | solution.py:12
  102.3 5.2 %all-gather.3 = f32[4,1,384]{2,1,0:T(1,128)S(1)} all-gather(f32[1,1,384]{2,1,0:T(1,128)S(1)} %reshape.265), channel_id=2, replica_groups=mesh['grp'=4,'dev'=8] {'grp'}, dimensions={0}, use_global_device_ids=true | all-gather | bytes 7680 | tf_op jit(solution)/shard_map/all_gather | solution.py:12
  108.4 2.1 convolution_multiply_fusion.3
  111.9 110.6 %while.69 = (s32[]{:T(128)}, f32[384,1024]{1,0:T(8,128)S(1)}, f32[128,1024]{1,0:T(8,128)}, s32[]{:T(128)}, s32[3,8]{0,1:T(8,128)S(1)}, /*index=5*/f32[8,384,128]...) while((s32[]{:T(128)}, f32[384,1024]{1,0:T(8,128)S(1)}, ...), condition=%wide.region_11.12_spmd, body=%wide.region_10.11_spmd.sunk | while | flops 202965152 | bytes 8528964 | solution.py:140
  114.7 14.3 %collective-permute-done.1 = f32[128,1024]{1,0:T(8,128)S(1)} collective-permute-done((f32[128,1024]{1,0:T(8,128)}, f32[128,1024]{1,0:T(8,128)S(1)}, u32[]{:S(2)}, u32[]{:S(2)}) %collective-permute-start.1) | collective-permute-done | bytes 524320 | tf_op jit(solution)/shard_map/while/body/eval_jaxpr/ppermute | solution.py:23
  133.0 13.6 %collective-permute-done.1 = f32[128,1024]{1,0:T(8,128)S(1)} collective-permute-done((f32[128,1024]{1,0:T(8,128)}, f32[128,1024]{1,0:T(8,128)S(1)}, u32[]{:S(2)}, u32[]{:S(2)}) %collective-permute-start.1) | collective-permute-done | bytes 524320 | tf_op jit(solution)/shard_map/while/body/eval_jaxpr/ppermute | solution.py:23
  150.6 12.7 %collective-permute-done.1 = f32[128,1024]{1,0:T(8,128)S(1)} collective-permute-done((f32[128,1024]{1,0:T(8,128)}, f32[128,1024]{1,0:T(8,128)S(1)}, u32[]{:S(2)}, u32[]{:S(2)}) %collective-permute-start.1) | collective-permute-done | bytes 524320 | tf_op jit(solution)/shard_map/while/body/eval_jaxpr/ppermute | solution.py:23
  167.2 11.7 %collective-permute-done.1 = f32[128,1024]{1,0:T(8,128)S(1)} collective-permute-done((f32[128,1024]{1,0:T(8,128)}, f32[128,1024]{1,0:T(8,128)S(1)}, u32[]{:S(2)}, u32[]{:S(2)}) %collective-permute-start.1) | collective-permute-done | bytes 524320 | tf_op jit(solution)/shard_map/while/body/eval_jaxpr/ppermute | solution.py:23
  183.0 10.8 %collective-permute-done.1 = f32[128,1024]{1,0:T(8,128)S(1)} collective-permute-done((f32[128,1024]{1,0:T(8,128)}, f32[128,1024]{1,0:T(8,128)S(1)}, u32[]{:S(2)}, u32[]{:S(2)}) %collective-permute-start.1) | collective-permute-done | bytes 524320 | tf_op jit(solution)/shard_map/while/body/eval_jaxpr/ppermute | solution.py:23
  197.8 9.9 %collective-permute-done.1 = f32[128,1024]{1,0:T(8,128)S(1)} collective-permute-done((f32[128,1024]{1,0:T(8,128)}, f32[128,1024]{1,0:T(8,128)S(1)}, u32[]{:S(2)}, u32[]{:S(2)}) %collective-permute-start.1) | collective-permute-done | bytes 524320 | tf_op jit(solution)/shard_map/while/body/eval_jaxpr/ppermute | solution.py:23
  211.7 9.4 %collective-permute-done.1 = f32[128,1024]{1,0:T(8,128)S(1)} collective-permute-done((f32[128,1024]{1,0:T(8,128)}, f32[128,1024]{1,0:T(8,128)S(1)}, u32[]{:S(2)}, u32[]{:S(2)}) %collective-permute-start.1) | collective-permute-done | bytes 524320 | tf_op jit(solution)/shard_map/while/body/eval_jaxpr/ppermute | solution.py:23
  222.5 3.4 %collective-permute-done.2 = f32[384,1024]{1,0:T(8,128)S(1)} collective-permute-done((f32[384,1024]{1,0:T(8,128)S(1)}, f32[384,1024]{1,0:T(8,128)S(1)}, u32[]{:S(2)}, u32[]{:S(2)}) %collective-permute-start.2) | collective-permute-done | bytes 1572896 | tf_op jit(solution)/shard_map/ppermute | solution.py:144
  227.3 16.4 %collective-permute-done.4 = f32[128,1024]{1,0:T(8,128)S(1)} collective-permute-done((f32[128,1024]{1,0:T(8,128)S(1)}, f32[128,1024]{1,0:T(8,128)S(1)}, u32[]{:S(2)}, u32[]{:S(2)}) %collective-permute-start.4) | collective-permute-done | bytes 524320 | tf_op jit(solution)/shard_map/ppermute | solution.py:23
  243.7 19.0 %collective-permute-done.3 = f32[384,1024]{1,0:T(8,128)S(1)} collective-permute-done((f32[384,1024]{1,0:T(8,128)S(1)}, f32[384,1024]{1,0:T(8,128)S(1)}, u32[]{:S(2)}, u32[]{:S(2)}) %collective-permute-start.3) | collective-permute-done | bytes 1572896 | tf_op jit(solution)/shard_map/ppermute | solution.py:144
  (197 shorter events, 56.2 us)
Async XLA Ops:
  0.6 5.0 %copy-start.3 = (s32[384]{0:T(512)S(1)}, s32[384]{0:T(512)}, u32[]{:S(2)}) copy-start(s32[384]{0:T(512)} %param.17) | copy-start | bytes 4612
  4.0 3.0 %copy-start.2 = (bf16[128,1024]{1,0:T(8,128)(2,1)S(1)}, bf16[128,1024]{1,0:T(8,128)(2,1)}, u32[]{:S(2)}) copy-start(bf16[128,1024]{1,0:T(8,128)(2,1)} %param.15) | copy-start | bytes 786436
  7.0 1.1 copy-start
  8.2 12.5 %collective-permute-start = (bf16[128,1024]{1,0:T(8,128)(2,1)}, bf16[128,1024]{1,0:T(8,128)(2,1)S(1)}, u32[]{:S(2)}, u32[]{:S(2)}) collective-permute-start(bf16[128,1024]{1,0:T(8,128)(2,1)} %get-tuple-element.1277), channel_id=1, source_target_pairs={{0,1},{1,2},{2,3},{3,4},{4,5},{5,6},{6,7},{7,0},{8,9},{9,10},{10,1... | collective-permute-start | bytes 786440 | tf_op jit(solution)/shard_map/while/body/eval_jaxpr/ppermute | solution.py:23
  22.7 10.5 %collective-permute-start = (bf16[128,1024]{1,0:T(8,128)(2,1)}, bf16[128,1024]{1,0:T(8,128)(2,1)S(1)}, u32[]{:S(2)}, u32[]{:S(2)}) collective-permute-start(bf16[128,1024]{1,0:T(8,128)(2,1)} %get-tuple-element.1277), channel_id=1, source_target_pairs={{0,1},{1,2},{2,3},{3,4},{4,5},{5,6},{6,7},{7,0},{8,9},{9,10},{10,1... | collective-permute-start | bytes 786440 | tf_op jit(solution)/shard_map/while/body/eval_jaxpr/ppermute | solution.py:23
  35.1 9.5 %collective-permute-start = (bf16[128,1024]{1,0:T(8,128)(2,1)}, bf16[128,1024]{1,0:T(8,128)(2,1)S(1)}, u32[]{:S(2)}, u32[]{:S(2)}) collective-permute-start(bf16[128,1024]{1,0:T(8,128)(2,1)} %get-tuple-element.1277), channel_id=1, source_target_pairs={{0,1},{1,2},{2,3},{3,4},{4,5},{5,6},{6,7},{7,0},{8,9},{9,10},{10,1... | collective-permute-start | bytes 786440 | tf_op jit(solution)/shard_map/while/body/eval_jaxpr/ppermute | solution.py:23
  46.6 9.3 %collective-permute-start = (bf16[128,1024]{1,0:T(8,128)(2,1)}, bf16[128,1024]{1,0:T(8,128)(2,1)S(1)}, u32[]{:S(2)}, u32[]{:S(2)}) collective-permute-start(bf16[128,1024]{1,0:T(8,128)(2,1)} %get-tuple-element.1277), channel_id=1, source_target_pairs={{0,1},{1,2},{2,3},{3,4},{4,5},{5,6},{6,7},{7,0},{8,9},{9,10},{10,1... | collective-permute-start | bytes 786440 | tf_op jit(solution)/shard_map/while/body/eval_jaxpr/ppermute | solution.py:23
  58.0 9.3 %collective-permute-start = (bf16[128,1024]{1,0:T(8,128)(2,1)}, bf16[128,1024]{1,0:T(8,128)(2,1)S(1)}, u32[]{:S(2)}, u32[]{:S(2)}) collective-permute-start(bf16[128,1024]{1,0:T(8,128)(2,1)} %get-tuple-element.1277), channel_id=1, source_target_pairs={{0,1},{1,2},{2,3},{3,4},{4,5},{5,6},{6,7},{7,0},{8,9},{9,10},{10,1... | collective-permute-start | bytes 786440 | tf_op jit(solution)/shard_map/while/body/eval_jaxpr/ppermute | solution.py:23
  69.3 9.3 %collective-permute-start = (bf16[128,1024]{1,0:T(8,128)(2,1)}, bf16[128,1024]{1,0:T(8,128)(2,1)S(1)}, u32[]{:S(2)}, u32[]{:S(2)}) collective-permute-start(bf16[128,1024]{1,0:T(8,128)(2,1)} %get-tuple-element.1277), channel_id=1, source_target_pairs={{0,1},{1,2},{2,3},{3,4},{4,5},{5,6},{6,7},{7,0},{8,9},{9,10},{10,1... | collective-permute-start | bytes 786440 | tf_op jit(solution)/shard_map/while/body/eval_jaxpr/ppermute | solution.py:23
  80.6 9.3 %collective-permute-start = (bf16[128,1024]{1,0:T(8,128)(2,1)}, bf16[128,1024]{1,0:T(8,128)(2,1)S(1)}, u32[]{:S(2)}, u32[]{:S(2)}) collective-permute-start(bf16[128,1024]{1,0:T(8,128)(2,1)} %get-tuple-element.1277), channel_id=1, source_target_pairs={{0,1},{1,2},{2,3},{3,4},{4,5},{5,6},{6,7},{7,0},{8,9},{9,10},{10,1... | collective-permute-start | bytes 786440 | tf_op jit(solution)/shard_map/while/body/eval_jaxpr/ppermute | solution.py:23
  92.0 16.5 %copy-start.1 = (bf16[8,128,1024]{2,1,0:T(8,128)(2,1)}, bf16[8,128,1024]{2,1,0:T(8,128)(2,1)S(1)}, u32[]{:S(2)}) copy-start(bf16[8,128,1024]{2,1,0:T(8,128)(2,1)S(1)} %get-tuple-element.1351) | copy-start | bytes 6291460
  111.9 17.1 %collective-permute-start.1 = (f32[128,1024]{1,0:T(8,128)}, f32[128,1024]{1,0:T(8,128)S(1)}, u32[]{:S(2)}, u32[]{:S(2)}) collective-permute-start(f32[128,1024]{1,0:T(8,128)} %get-tuple-element.1361), channel_id=1, source_target_pairs={{0,1},{1,2},{2,3},{3,4},{4,5},{5,6},{6,7},{7,0},{8,9},{9,10},{10,1... | collective-permute-start | bytes 1572872 | tf_op jit(solution)/shard_map/while/body/eval_jaxpr/ppermute | solution.py:23
  130.3 16.2 %collective-permute-start.1 = (f32[128,1024]{1,0:T(8,128)}, f32[128,1024]{1,0:T(8,128)S(1)}, u32[]{:S(2)}, u32[]{:S(2)}) collective-permute-start(f32[128,1024]{1,0:T(8,128)} %get-tuple-element.1361), channel_id=1, source_target_pairs={{0,1},{1,2},{2,3},{3,4},{4,5},{5,6},{6,7},{7,0},{8,9},{9,10},{10,1... | collective-permute-start | bytes 1572872 | tf_op jit(solution)/shard_map/while/body/eval_jaxpr/ppermute | solution.py:23
  147.9 15.3 %collective-permute-start.1 = (f32[128,1024]{1,0:T(8,128)}, f32[128,1024]{1,0:T(8,128)S(1)}, u32[]{:S(2)}, u32[]{:S(2)}) collective-permute-start(f32[128,1024]{1,0:T(8,128)} %get-tuple-element.1361), channel_id=1, source_target_pairs={{0,1},{1,2},{2,3},{3,4},{4,5},{5,6},{6,7},{7,0},{8,9},{9,10},{10,1... | collective-permute-start | bytes 1572872 | tf_op jit(solution)/shard_map/while/body/eval_jaxpr/ppermute | solution.py:23
  164.6 14.4 %collective-permute-start.1 = (f32[128,1024]{1,0:T(8,128)}, f32[128,1024]{1,0:T(8,128)S(1)}, u32[]{:S(2)}, u32[]{:S(2)}) collective-permute-start(f32[128,1024]{1,0:T(8,128)} %get-tuple-element.1361), channel_id=1, source_target_pairs={{0,1},{1,2},{2,3},{3,4},{4,5},{5,6},{6,7},{7,0},{8,9},{9,10},{10,1... | collective-permute-start | bytes 1572872 | tf_op jit(solution)/shard_map/while/body/eval_jaxpr/ppermute | solution.py:23
  180.3 13.5 %collective-permute-start.1 = (f32[128,1024]{1,0:T(8,128)}, f32[128,1024]{1,0:T(8,128)S(1)}, u32[]{:S(2)}, u32[]{:S(2)}) collective-permute-start(f32[128,1024]{1,0:T(8,128)} %get-tuple-element.1361), channel_id=1, source_target_pairs={{0,1},{1,2},{2,3},{3,4},{4,5},{5,6},{6,7},{7,0},{8,9},{9,10},{10,1... | collective-permute-start | bytes 1572872 | tf_op jit(solution)/shard_map/while/body/eval_jaxpr/ppermute | solution.py:23
  195.1 12.5 %collective-permute-start.1 = (f32[128,1024]{1,0:T(8,128)}, f32[128,1024]{1,0:T(8,128)S(1)}, u32[]{:S(2)}, u32[]{:S(2)}) collective-permute-start(f32[128,1024]{1,0:T(8,128)} %get-tuple-element.1361), channel_id=1, source_target_pairs={{0,1},{1,2},{2,3},{3,4},{4,5},{5,6},{6,7},{7,0},{8,9},{9,10},{10,1... | collective-permute-start | bytes 1572872 | tf_op jit(solution)/shard_map/while/body/eval_jaxpr/ppermute | solution.py:23
  209.0 12.1 %collective-permute-start.1 = (f32[128,1024]{1,0:T(8,128)}, f32[128,1024]{1,0:T(8,128)S(1)}, u32[]{:S(2)}, u32[]{:S(2)}) collective-permute-start(f32[128,1024]{1,0:T(8,128)} %get-tuple-element.1361), channel_id=1, source_target_pairs={{0,1},{1,2},{2,3},{3,4},{4,5},{5,6},{6,7},{7,0},{8,9},{9,10},{10,1... | collective-permute-start | bytes 1572872 | tf_op jit(solution)/shard_map/while/body/eval_jaxpr/ppermute | solution.py:23
  222.5 4.8 %copy-start.4 = (f32[128,1024]{1,0:T(8,128)S(1)}, f32[128,1024]{1,0:T(8,128)}, u32[]{:S(2)}) copy-start(f32[128,1024]{1,0:T(8,128)} %get-tuple-element.938) | copy-start | bytes 1572868
  222.5 3.4 %collective-permute-start.2 = (f32[384,1024]{1,0:T(8,128)S(1)}, f32[384,1024]{1,0:T(8,128)S(1)}, u32[]{:S(2)}, u32[]{:S(2)}) collective-permute-start(f32[384,1024]{1,0:T(8,128)S(1)} %get-tuple-element.937), channel_id=1, source_target_pairs={{0,8},{8,0},{16,24},{24,16},{1,9},{9,1},{17,25},{25,17},{2,10},{10... | collective-permute-start | bytes 4718600 | tf_op jit(solution)/shard_map/ppermute | solution.py:144
  226.2 36.5 %collective-permute-start.3 = (f32[384,1024]{1,0:T(8,128)S(1)}, f32[384,1024]{1,0:T(8,128)S(1)}, u32[]{:S(2)}, u32[]{:S(2)}) collective-permute-start(f32[384,1024]{1,0:T(8,128)S(1)} %add.366), channel_id=1, source_target_pairs={{0,16},{8,24},{16,0},{24,8},{1,17},{9,25},{17,1},{25,9},{2,18},{10... | collective-permute-start | bytes 4718600 | tf_op jit(solution)/shard_map/ppermute | solution.py:144
  227.3 16.4 %collective-permute-start.4 = (f32[128,1024]{1,0:T(8,128)S(1)}, f32[128,1024]{1,0:T(8,128)S(1)}, u32[]{:S(2)}, u32[]{:S(2)}) collective-permute-start(f32[128,1024]{1,0:T(8,128)S(1)} %copy-done.4), channel_id=1, source_target_pairs={{0,1},{1,2},{2,3},{3,4},{4,5},{5,6},{6,7},{7,0},{8,9},{9,10},{10,1... | collective-permute-start | bytes 1572872 | tf_op jit(solution)/shard_map/ppermute | solution.py:23
